TPU v7x, 32 devices: a whole 2x2x4 slice. The times are simulated.
32 devices in a mesh: groups: 2 (over x), ctx: 2 (over core), fsdp: 8 (over z, y).
Axes of the slice: x: 2, y: 2, z: 4, core: 2. Of those that a mesh axis runs over, the one named last changes fastest.
Arguments:
- hidden_in: bfloat16 [8192, 2048], P(('groups', 'ctx', 'fsdp')), parts along dimension 0, may hold values from -6 to 6
- qkv_weight: bfloat16 [2048, 4096], P(None, 'fsdp'), may hold values from -0.125 to 0.125
- ab_weight: bfloat16 [2048, 32], replicated, may hold values from -0.125 to 0.125
- conv_weight: float32 [4, 4096], replicated, may hold values from -3 to 3
- decay_rate: float32 [16], replicated, may hold values from 7.324219e-05 to 0.3
- dt_bias: float32 [16], replicated, may hold values from -3 to -1
- norm_gain: float32 [128], replicated, may hold values from 0.1 to 1.9
- previous_tail: bfloat16 [6, 4096], P('groups'), parts along dimension 0, may hold values from -6 to 6
- window_entry_state: float32 [32, 128, 128], P('groups'), parts along dimension 0, may hold values from -3 to 3
Outputs:
- head_out: bfloat16 [8192, 2048], P(('groups', 'ctx', 'fsdp')), parts along dimension 0
There are 2 independent parts, one for each index of `groups`. A program takes and returns all parts, laid end to end along the dimension named above; an argument that names none is the same for every part. Nothing has to cross between parts.
All inputs are finite; a program needn't handle non-finite values.
Results may differ from a plain program's by a relative error of at most 0.0065.
Values may be sent and summed in bfloat16 or wider, within the bound.
A program may use at most 320 MiB of HBM per device.

v0:
```python
import jax
import jax.numpy as jnp
from jax import lax
from jax.sharding import PartitionSpec as P

HK = 8
HV = 16
DK = 128
DV = 128
SPAN = 64


exact_product = lax.Precision.HIGHEST


def shifted(array, axis, by):
    peers = lax.axis_size(axis)
    pairs = [(i, i + by) for i in range(peers) if 0 <= i + by < peers]
    return lax.ppermute(array, axis, pairs)


def entering(part, axis, combine, identity):
    place = lax.axis_index(axis)
    gathered = jax.tree.map(lambda a: lax.all_gather(a, axis), part)
    state = jax.tree.map(lambda a, e: jnp.zeros_like(a) + jnp.asarray(e, a.dtype), part, identity)

    def one(hop, state):
        return combine(
            state, jax.tree.map(lambda a: lax.dynamic_index_in_dim(a, hop, 0, False), gathered)
        )

    return lax.fori_loop(0, place, one, state)


def unit_norm(vectors):
    return vectors * lax.rsqrt(jnp.sum(vectors * vectors, axis=-1, keepdims=True) + 1e-06)


def convolve(before, mixed_qkv, conv_weight):
    length = mixed_qkv.shape[0]
    padded = jnp.concatenate([before, mixed_qkv], axis=0).astype(jnp.float32)
    summed = jnp.zeros((length, mixed_qkv.shape[1]), jnp.float32)
    for offset in range(conv_weight.shape[0]):
        summed = summed + conv_weight[offset] * padded[offset : offset + length]
    return jax.nn.silu(summed)


def to_spans(tensor, span_len):
    length, head_count = (tensor.shape[0], tensor.shape[1])
    shaped = tensor.reshape((length // span_len, span_len, head_count) + tensor.shape[2:])
    return jnp.moveaxis(shaped, 2, 1)


def head_inputs(conv_out, gate_logits, decay_rate, dt_bias):
    length = conv_out.shape[0]
    queries = unit_norm(conv_out[:, : HK * DK].reshape(length, HK, DK)) * DK ** (-0.5)
    head_keys = unit_norm(conv_out[:, HK * DK : 2 * HK * DK].reshape(length, HK, DK))
    values = conv_out[:, 2 * HK * DK :].reshape(length, HV, DV)
    queries = jnp.repeat(queries, HV // HK, axis=1)
    head_keys = jnp.repeat(head_keys, HV // HK, axis=1)
    write_rate = jax.nn.sigmoid(gate_logits[:, HV:])
    logdecay = -decay_rate * jax.nn.softplus(gate_logits[:, :HV] + dt_bias)
    return [to_spans(item, SPAN) for item in (queries, head_keys, values, write_rate, logdecay)]


def lower_inverse(strict_part):
    span_len = strict_part.shape[-1]
    unit_span = jnp.eye(span_len, dtype=strict_part.dtype)
    inverse = unit_span - strict_part
    power = strict_part
    reach = 2
    while reach < span_len:
        power = jnp.einsum("...ij,...jk->...ik", power, power, precision=exact_product)
        inverse = inverse + jnp.einsum(
            "...ij,...jk->...ik", inverse, power, precision=exact_product
        )
        reach = reach * 2
    return inverse


def span_terms(queries, head_keys, values, write_rate, logdecay):
    span_len = logdecay.shape[-1]
    cumulative = jnp.cumsum(logdecay, axis=-1)
    row_index = lax.broadcasted_iota(jnp.int32, (span_len, span_len), 0)
    col_index = lax.broadcasted_iota(jnp.int32, (span_len, span_len), 1)
    lower_mask = row_index >= col_index
    gap_log = cumulative[..., :, None] - cumulative[..., None, :]
    factor = jnp.where(lower_mask, jnp.exp(jnp.where(lower_mask, gap_log, 0.0)), 0.0)
    strict = jnp.where(row_index > col_index, factor, 0.0)
    key_products = jnp.einsum("...ik,...jk->...ij", head_keys, head_keys, precision=exact_product)
    query_products = jnp.einsum("...ik,...jk->...ij", queries, head_keys, precision=exact_product)
    inverse = lower_inverse(write_rate[..., :, None] * key_products * strict)
    growth = jnp.exp(cumulative)
    right_sides = jnp.concatenate(
        [write_rate[..., None] * values, (write_rate * growth)[..., None] * head_keys], axis=-1
    )
    solved = jnp.einsum("...ij,...jc->...ic", inverse, right_sides, precision=exact_product)
    new_values = solved[..., : values.shape[-1]]
    key_weights = solved[..., values.shape[-1] :]
    scores = query_products * factor
    window_local_output = jnp.einsum(
        "...ij,...jv->...iv", scores, new_values, precision=exact_product
    )
    effective_query = growth[..., None] * queries - jnp.einsum(
        "...ij,...jk->...ik", scores, key_weights, precision=exact_product
    )
    span_end = cumulative[..., -1]
    tail_decay = jnp.exp(span_end[..., None] - cumulative)
    decayed_keys = head_keys * tail_decay[..., None]
    unit_key = jnp.eye(head_keys.shape[-1], dtype=logdecay.dtype)
    state_mapping = jnp.exp(span_end)[..., None, None] * unit_key - jnp.einsum(
        "...ck,...cj->...kj", decayed_keys, key_weights, precision=exact_product
    )
    shifted_state = jnp.einsum(
        "...ck,...cv->...kv", decayed_keys, new_values, precision=exact_product
    )
    return (effective_query, window_local_output, state_mapping, shifted_state)


def finish(result_rows, norm_gain):
    mean_square = jnp.mean(result_rows * result_rows, axis=-1, keepdims=True)
    normed = result_rows * lax.rsqrt(mean_square + 1e-06) * norm_gain
    normed = jnp.moveaxis(normed, 1, 2)
    return normed.reshape(
        normed.shape[0] * normed.shape[1], normed.shape[2] * normed.shape[3]
    ).astype(jnp.bfloat16)


def compose(former_piece, latter_piece):
    joined_map = jnp.einsum(
        "hkj,hjm->hkm", latter_piece[0], former_piece[0], precision=exact_product
    )
    combined_state = (
        jnp.einsum("zom,zmg->zog", latter_piece[0], former_piece[1], precision=exact_product)
        + latter_piece[1]
    )
    return (joined_map, combined_state)


def shards(
    hidden_in,
    qkv_weight,
    ab_weight,
    conv_weight,
    decay_rate,
    dt_bias,
    norm_gain,
    previous_tail,
    window_entry_state,
):
    mixed_qkv = jnp.dot(
        hidden_in,
        lax.all_gather(qkv_weight, "fsdp", axis=1, tiled=True),
        preferred_element_type=jnp.float32,
    ).astype(jnp.bfloat16)
    gate_logits = jnp.dot(hidden_in, ab_weight, preferred_element_type=jnp.float32)
    tail_rows = previous_tail.shape[0]
    received = shifted(mixed_qkv[mixed_qkv.shape[0] - tail_rows :], ("ctx", "fsdp"), 1)
    before = jnp.where(lax.axis_index(("ctx", "fsdp")) == 0, previous_tail, received)
    conv_out = convolve(before, mixed_qkv, conv_weight)
    spanned = head_inputs(conv_out, gate_logits, decay_rate, dt_bias)
    effective_query, window_local_output, state_mapping, shifted_state = span_terms(*spanned)
    unit_maps = jnp.broadcast_to(jnp.eye(DK, dtype=jnp.float32), (HV, DK, DK))
    empty_state = jnp.zeros((HV, DK, DV), jnp.float32)

    def advance(carried, items):
        carry_map, carried_over_state = carried
        per_step_query, per_step_local, per_step_mapping, step_offset = items
        adjusted_result = jnp.einsum(
            "hck,hkj->hcj", per_step_query, carry_map, precision=exact_product
        )
        layer_result = per_step_local + jnp.einsum(
            "gpi,gib->gpb", per_step_query, carried_over_state, precision=exact_product
        )
        carry_map = jnp.einsum("hkj,hjm->hkm", per_step_mapping, carry_map, precision=exact_product)
        carried_over_state = (
            jnp.einsum(
                "zom,zmg->zog", per_step_mapping, carried_over_state, precision=exact_product
            )
            + step_offset
        )
        return ((carry_map, carried_over_state), (adjusted_result, layer_result))

    own_pair, (adjusted_result, incomplete_output) = lax.scan(
        advance,
        (unit_maps, empty_state),
        (effective_query, window_local_output, state_mapping, shifted_state),
    )
    identity = (unit_maps, empty_state)
    leading_pair = entering((own_pair[0], own_pair[1]), ("ctx", "fsdp"), compose, identity)
    opening_state = (
        jnp.einsum("zom,zmg->zog", leading_pair[0], window_entry_state, precision=exact_product)
        + leading_pair[1]
    )
    result_rows = incomplete_output + jnp.einsum(
        "elfx,lxw->elfw", adjusted_result, opening_state, precision=exact_product
    )
    return finish(result_rows, norm_gain)


def solution(mesh):
    placed = (
        P(("groups", "ctx", "fsdp"), None),
        P(None, "fsdp"),
        P(),
        P(),
        P(),
        P(),
        P(),
        P("groups", None),
        P("groups", None, None),
    )
    return jax.shard_map(
        shards,
        mesh=mesh,
        in_specs=placed,
        out_specs=P(("groups", "ctx", "fsdp"), None),
        check_vma=False,
    )
```

profile of v0, /device:TPU:31, one launch (start us, length us, event | category | flops | bytes accessed | tf_op | source)
XLA Modules:
  0.0 710.3 jit_solution(9324896033051884628)
XLA Ops:
  9.7 225.8 %all-gather.6.cloned.1.call-done = bf16[2048,4096]{1,0:T(8,128)(2,1)} async-done(((bf16[2048,512]{1,0:T(8,128)(2,1)}), bf16[2048,4096]{1,0:T(8,128)(2,1)}) %all-gather.6.cloned.1.call-update) | async-done | bytes 16777232 | tf_op jit(solution)/shard_map/all_gather | solution.py:153
  235.5 8.4 %convolution_convert_fusion = bf16[256,4096]{1,0:T(8,128)(2,1)S(1)} fusion(bf16[256,2048]{1,0:T(8,128)(2,1)S(1)} %copy-done, bf16[2048,4096]{1,0:T(8,128)(2,1)} %all-gather.6.cloned.1.call-done), kind=kOutput, calls=%fused_computation.35 | convolution fusion | flops 4296015872 | bytes 19922944 | tf_op jit(solution)/shard_map/dot_general | solution.py:151
  246.5 3.0 collective-permute-done
  250.9 2.8 divide_multiply_fusion
  257.3 3.5 fusion.45
  260.8 3.6 select_multiply_fusion
  266.6 2.7 fusion.88
  289.3 4.5 fusion.34
  293.8 3.6 fusion.47
  297.4 3.9 fusion.40
  301.4 8.9 %fusion.46 = f32[4,16,128,128]{3,2,1,0:T(8,128)} fusion(f32[4,16,64,256]{3,2,1,0:T(8,128)S(1)} %fusion.34, f32[4,64,16,128]{3,1,0,2:T(8,128)S(1)} %bitcast.166, f32[4,16,64]{2,1,0:T(8,128)S(1)} %get-tuple-element.163), kind=kOutput, calls=%fused_computation.68 | convolution fusion | flops 805830656 | bytes 8421376 | tf_op jit(solution)/shard_map/...ck,...cv->...kv/dot_general | solution.py:114
  310.2 9.7 %multiply_subtract_fusion = f32[4,16,128,128]{3,2,1,0:T(8,128)} fusion(f32[128,128]{1,0:T(8,128)S(1)} %fusion.76, f32[4,16]{1,0:T(4,128)S(1)} %exp.36, f32[4,16,64,256]{3,2,1,0:T(8,128)S(1)} %fusion.34, f32[4,64,16,128]{3,1,0,2:T(8,128)S(1)} %bitcast.167, f32[4,16,64]{2,1,0:T(8,128)S(1)} %get-tuple-element.163), kind=kOutput, calls=%fused_computation.48 | convolution fusion | flops 807927808 | bytes 8488960 | tf_op jit(solution)/shard_map/...ck,...cj->...kj/dot_general | solution.py:111
  320.0 39.9 %while.30 = (s32[]{:T(128)}, f32[16,128,128]{2,1,0:T(8,128)S(1)}, f32[16,128,128]{2,1,0:T(8,128)S(1)}, f32[4,16,64,128]{3,2,0,1:T(8,128)}, f32[4,16,64,128]{3,2,...) while((s32[]{:T(128)}, f32[16,128,128]{2,1,0:T(8,128)S(1)}, ...), condition=%wide.region_4.5_spmd.clone, body=%wide.region_3.4_spmd.clone.sunk | while | flops 1208877056 | bytes 41423032 | solution.py:184
  324.7 2.9 fusion.157
  334.6 2.9 fusion.157
  344.6 2.9 fusion.157
  354.6 2.9 fusion.157
  361.7 126.7 %all-gather.8.cloned.1.call-done = f32[256,128,128]{2,1,0:T(8,128)} async-done(((f32[16,128,128]{2,1,0:T(8,128)}), f32[256,128,128]{2,1,0:T(8,128)}) %all-gather.8.cloned.1.call-update) | async-done | bytes 16777232 | tf_op jit(solution)/shard_map/all_gather | solution.py:24
  488.4 127.3 %all-gather.10.cloned.1.call-done = f32[256,128,128]{2,1,0:T(8,128)} async-done(((f32[16,128,128]{2,1,0:T(8,128)}), f32[256,128,128]{2,1,0:T(8,128)}) %all-gather.10.cloned.1.call-update) | async-done | bytes 16777232 | tf_op jit(solution)/shard_map/all_gather | solution.py:24
  615.9 80.2 %while.29 = (s32[]{:T(128)}, f32[16,128,128]{2,1,0:T(8,128)S(1)}, f32[16,128,128]{2,1,0:T(8,128)S(1)}, s32[]{:T(128)}, f32[16,16,128,128]{3,2,1,0:T(8,128)}, /*i...) while((s32[]{:T(128)}, f32[16,128,128]{2,1,0:T(8,128)S(1)}, ...), condition=%wide.region_6.7_spmd, body=%wide.region_5.6_spmd.sunk | while | flops 805568512 | bytes 11535499 | solution.py:32
  616.1 2.8 convolution_add_fusion.8
  653.5 2.7 convolution_add_fusion.8
  658.8 2.8 convolution_add_fusion.8
  680.2 2.7 convolution_add_fusion.8
  (182 shorter events, 138.0 us)
Async XLA Ops:
  6.5 1.2 copy-start
  6.5 1.2 copy-start.9
  6.5 1.7 copy-start.13
  6.5 3.1 copy-start.10
  6.5 228.9 %all-gather.6.cloned.1.call-start = ((), (), s32[]{:S(2)}) async-start(), calls=%async_computation | async-start | bytes 18874368 | tf_op jit(solution)/shard_map/all_gather | solution.py:153
  7.3 481.1 %all-gather.8.cloned.1.call-start = ((), (), s32[]{:S(2)}) async-start(), calls=%async_computation.1 | async-start | bytes 17825792 | tf_op jit(solution)/shard_map/all_gather | solution.py:24
  9.7 239.8 %copy-start.11 = (bf16[3,4096]{1,0:T(4,128)(2,1)S(1)}, bf16[3,4096]{1,0:T(4,128)(2,1)}, u32[]{:S(2)}) copy-start(bf16[3,4096]{1,0:T(4,128)(2,1)} %param.20) | copy-start | bytes 73732
  244.5 5.0 collective-permute-start
  257.3 3.5 copy-start.12
  320.0 1.6 copy-start.5
  320.1 3.4 copy-start.2
  330.0 1.6 copy-start.5
  330.1 3.4 copy-start.2
  340.0 1.6 copy-start.5
  340.1 3.4 copy-start.2
  350.0 1.6 copy-start.5
  350.1 3.4 copy-start.2
  360.0 1.3 copy-start.4
  360.9 254.8 %all-gather.10.cloned.1.call-start = ((), (), s32[]{:S(2)}) async-start(), calls=%async_computation.2 | async-start | bytes 17825792 | tf_op jit(solution)/shard_map/all_gather | solution.py:24
  615.9 80.2 %copy-start.8 = (f32[16,128,128]{2,1,0:T(8,128)S(1)}, f32[16,128,128]{2,1,0:T(8,128)}, u32[]{:S(2)}) copy-start(f32[16,128,128]{2,1,0:T(8,128)} %param.21) | copy-start | bytes 3145732
  696.2 1.6 copy-start.6
  696.2 2.2 copy-start.7
  698.4 2.5 copy-start.14
  701.0 2.7 copy-start.1
  (2 other events, 1.8 us)
Sparse Core Ops, SparseCore 0:
  9.4 226.0 all-gather.5
  361.1 127.2 all-gather.7
  490.6 125.0 all-gather.9
where the time goes:
time: 716 us; the launch traced here: 710 us
  waiting for transfers between devices  484 us (68%)
  matrix products  184 us (26%)
  local copies, waits for them, and re-layouts  16.5 us (2%)
  between operations  13.8 us (2%)
  other arithmetic  9.23 us (1%)
    all_gather x2, waiting for transfers between devices, entering(): gathered = jax.tree.map(lambda a: lax.all_gather(a, axis), part)  254 us
    all_gather x1, waiting for transfers between devices, shards(): lax.all_gather(qkv_weight, 'fsdp', axis=1, tiled=True)  226 us
    dot_general x15, matrix products, compose(): jnp.einsum('zom,zmg->zog', latter_piece[0], former_piece[1], precision=ex...  40.7 us
    dot_general x15, matrix products, compose(): jnp.einsum('hkj,hjm->hkm', latter_piece[0], former_piece[0], precision=ex...  36.3 us
  transfers between devices with their start and end apart: 4, of which 4 were waited for; matrix products, arithmetic and copies ran while one was open for 0% of the time, Pallas kernels for 0%

commit v1 on v0

v1 whole, which is shorter than its diff:
```python
import jax
import jax.numpy as jnp
from jax import lax
from jax.experimental import pallas as pl
from jax.experimental.pallas import tpu as pltpu
from jax.sharding import PartitionSpec as P

HK = 8
HV = 16
DK = 128
DV = 128
BLOCK = 512
CHUNK = 128
BASE = 32


def mm(a, b):
    return jnp.dot(a.astype(jnp.bfloat16), b.astype(jnp.bfloat16), preferred_element_type=jnp.float32)


def mm_nt(a, b):
    return lax.dot_general(
        a.astype(jnp.bfloat16),
        b.astype(jnp.bfloat16),
        (((1,), (1,)), ((), ())),
        preferred_element_type=jnp.float32,
    )


def mm_tn(a, b):
    return lax.dot_general(
        a.astype(jnp.bfloat16),
        b.astype(jnp.bfloat16),
        (((0,), (0,)), ((), ())),
        preferred_element_type=jnp.float32,
    )


def unit_lower_inverses(parts, row, col):
    eye = jnp.where(row == col, 1.0, 0.0)
    near = (row // BASE) == (col // BASE)
    powers = [jnp.where(near, a, 0.0) for a in parts]
    inverses = [eye - p for p in powers]
    reach = 2
    while reach < BASE:
        powers = [mm(p, p) for p in powers]
        inverses = [x + mm(x, p) for x, p in zip(inverses, powers)]
        reach *= 2
    size = BASE
    while size < CHUNK:
        joined = ((row // (2 * size)) == (col // (2 * size))) & ((row // size) != (col // size))
        sides = [mm(x, jnp.where(joined, a, 0.0)) for x, a in zip(inverses, parts)]
        inverses = [x - mm(y, x) for x, y in zip(inverses, sides)]
        size *= 2
    return inverses


def layer_kernel(hid_ref, w_ref, taps_ref, scal_ref, tail_ref, entry_ref, out_ref, buf, state):
    step = pl.program_id(0)

    @pl.when(step == 0)
    def _():
        state[...] = entry_ref[...]
        buf[0:8, :] = tail_ref[...]

    block = hid_ref.shape[0]
    wide = 3 * DK
    product = jnp.dot(hid_ref[...], w_ref[...], preferred_element_type=jnp.float32)
    buf[8 : 8 + block, :] = product[:, :wide].astype(jnp.bfloat16).astype(jnp.float32)
    summed = taps_ref[0:1, :] * buf[5 : 5 + block, :]
    for j in range(1, 4):
        summed = summed + taps_ref[j : j + 1, :] * buf[5 + j : 5 + j + block, :]
    buf[0:8, :] = buf[block : block + 8, :]
    conv = summed / (1.0 + jnp.exp(-summed))
    q = conv[:, :DK]
    k = conv[:, DK : 2 * DK]
    v = conv[:, 2 * DK :]
    q = q * (lax.rsqrt(jnp.sum(q * q, axis=-1, keepdims=True) + 1e-06) * DK ** (-0.5))
    k = k * lax.rsqrt(jnp.sum(k * k, axis=-1, keepdims=True) + 1e-06)

    spans = block // CHUNK
    row = lax.broadcasted_iota(jnp.int32, (CHUNK, CHUNK), 0)
    col = lax.broadcasted_iota(jnp.int32, (CHUNK, CHUNK), 1)
    low = row >= col
    upper = jnp.where(row <= col, 1.0, 0.0)
    logits = jnp.transpose(product[:, wide:], (1, 0))[0:8, :]
    shifted_logit = logits[0:1, :] + scal_ref[1:2, 0:1]
    softplus = jnp.maximum(shifted_logit, 0.0) + jnp.log1p(jnp.exp(-jnp.abs(shifted_logit)))
    logdecay = -scal_ref[0:1, 0:1] * softplus
    rate = 1.0 / (1.0 + jnp.exp(-logits[1:2, :]))
    decays = jnp.concatenate(
        [logdecay[:, i * CHUNK : (i + 1) * CHUNK] for i in range(spans)]
        + [jnp.zeros((8 - spans, CHUNK), jnp.float32)] * (1 if spans < 8 else 0),
        axis=0,
    )
    sums = jnp.dot(decays, upper, precision=lax.Precision.HIGHEST, preferred_element_type=jnp.float32)

    ks, qs, parts, scores, rights, ends, tails = [], [], [], [], [], [], []
    for i in range(spans):
        part = slice(i * CHUNK, (i + 1) * CHUNK)
        ki, qi, vi = k[part], q[part], v[part]
        cs = sums[i : i + 1, :]
        beta = rate[:, part]
        end = cs[:, CHUNK - 1 : CHUNK]
        growth = jnp.exp(cs)
        rows = jnp.concatenate(
            [cs, beta, growth, beta * growth, jnp.exp(end - cs), jnp.zeros((CHUNK - 5, CHUNK), jnp.float32)], axis=0
        )
        cols = jnp.transpose(rows, (1, 0))
        gap = cols[:, 0:1] - cs
        factor = jnp.where(low, jnp.exp(jnp.where(low, gap, 0.0)), 0.0)
        both = mm_nt(jnp.concatenate([ki, qi], axis=0), ki)
        parts.append(jnp.where(row > col, cols[:, 1:2] * both[:CHUNK] * factor, 0.0))
        scores.append(both[CHUNK:] * factor)
        rights.append(jnp.concatenate([cols[:, 1:2] * vi, cols[:, 3:4] * ki], axis=1))
        qs.append(cols[:, 2:3] * qi)
        ks.append(ki * cols[:, 4:5])
        ends.append(jnp.exp(end))
    inverses = unit_lower_inverses(parts, row, col)
    solved = [mm(x, r) for x, r in zip(inverses, rights)]

    held = state[...]
    for i in range(spans):
        both = mm(jnp.concatenate([solved[i][:, DV:], qs[i]], axis=0), held)
        fresh = solved[i][:, :DV] - both[:CHUNK]
        result = both[CHUNK:] + mm(scores[i], fresh)
        held = ends[i] * held + mm_tn(ks[i], fresh)
        mean_square = jnp.mean(result * result, axis=-1, keepdims=True)
        out_ref[i * CHUNK : (i + 1) * CHUNK, :] = (
            result * lax.rsqrt(mean_square + 1e-06) * scal_ref[2:3, :]
        ).astype(jnp.bfloat16)
    state[...] = held


def layer(hidden, weights, taps, scal, tail, entry, interpret=False):
    tokens, width = hidden.shape
    full = lambda a: pl.BlockSpec(a.shape, lambda i: (0,) * a.ndim)
    return pl.pallas_call(
        layer_kernel,
        grid=(tokens // BLOCK,),
        in_specs=[pl.BlockSpec((BLOCK, width), lambda i: (i, 0))]
        + [full(a) for a in (weights, taps, scal, tail, entry)],
        out_specs=pl.BlockSpec((BLOCK, DV), lambda i: (i, 0)),
        out_shape=jax.ShapeDtypeStruct((tokens, DV), jnp.bfloat16),
        scratch_shapes=[pltpu.VMEM((BLOCK + 8, 3 * DK), jnp.float32), pltpu.VMEM((DK, DV), jnp.float32)],
        compiler_params=pltpu.CompilerParams(vmem_limit_bytes=48 * 1024 * 1024),
        interpret=interpret,
    )(hidden, weights, taps, scal, tail, entry)


def head_columns(array, own_qk, own_v):
    picks = (own_qk * DK, (HK + own_qk) * DK, 2 * HK * DK + own_v * DV)
    return jnp.concatenate([lax.dynamic_slice_in_dim(array, at, DK, 1) for at in picks], axis=1)


def ring_member(place, peers):
    late = place // (peers // 2)
    return 2 * place * (1 - late) + (2 * peers - 1 - 2 * place) * late


def exchange_kernel(
    hid_ref, shard_ref, gate_ref, all_ref, w_ref, ring_send, ring_recv, twin_send, twin_recv, local, w_send, w_recv, w_local
):
    c, f = lax.axis_index("ctx"), lax.axis_index("fsdp")
    peers = HK
    rows = hid_ref.shape[0]
    half = rows // 2
    place = (f // 2) * (1 - f % 2) + (peers - 1 - f // 2) * (f % 2)
    there = lambda cc, ff: {"ctx": cc, "fsdp": ff}
    barrier = pltpu.get_barrier_semaphore()
    for cc in range(2):
        for df in range(peers):
            if cc or df:
                pl.semaphore_signal(
                    barrier,
                    inc=1,
                    device_id=there((c + cc) % 2, (f + df) % peers),
                    device_id_type=pl.DeviceIdType.MESH,
                )
    pl.semaphore_wait(barrier, 2 * peers - 1)

    def remote(src, dst, send, recv, device):
        return pltpu.make_async_remote_copy(
            src_ref=src, dst_ref=dst, send_sem=send, recv_sem=recv, device_id=device, device_id_type=pl.DeviceIdType.MESH
        )

    def landing(member, start, size):
        return all_ref.at[pl.ds(pl.multiple_of((c * peers + member) * rows + start, half), size), :]

    def span(way, hop):
        return (0, rows) if hop < peers // 2 else ((0, half) if way == 0 else (half, half))

    def ring(way, hop):
        ahead = 1 if way == 0 else peers - 1
        target = ring_member((place + ahead) % peers, peers)
        origin = ring_member((place + (peers - ahead) * (hop - 1)) % peers, peers)
        start, size = span(way, hop)
        src = hid_ref.at[pl.ds(start, size), :] if hop == 1 else landing(origin, start, size)
        return remote(
            src, landing(origin, start, size), ring_send.at[way, hop - 1], ring_recv.at[way, hop - 1], there(c, target)
        )

    def twin(way, hop):
        ahead = 1 if way == 0 else peers - 1
        origin = ring_member((place + (peers - ahead) * hop) % peers, peers)
        block = landing(origin, *span(way, hop))
        at = 1 + way * (peers // 2) + hop - 1
        return remote(block, block, twin_send.at[at], twin_recv.at[at], there(1 - c, f))

    halves = shard_ref.shape[0] // 2

    def weight(i, qk):
        if qk:
            d = (HK // 2) * (f % 2) + i
            lines = pl.ds(pl.multiple_of(c * halves, halves), halves)
            src = shard_ref.at[lines, pl.ds(i * DK, DK)]
            dst = w_ref.at[lines, pl.ds(pl.multiple_of((f // 2) * DK, DK), DK)]
            sem = w_recv.at[f // 2]
        else:
            d = 2 * (f - 4) + i
            src = shard_ref.at[:, pl.ds(pl.multiple_of((2 * i + c) * DK, DK), DK)]
            dst = w_ref.at[:, pl.ds(2 * DK, DK)]
            sem = w_recv.at[2]
        return d, src, dst, sem

    def weights(finish):
        for qk, count in ((True, 4), (False, 2)):

            @pl.when((f < 4) if qk else (f >= 4))
            def _():
                for i in range(count):
                    d, src, dst, sem = weight(i, qk)

                    @pl.when(d != f)
                    def _():
                        far = remote(src, dst, w_send.at[i], sem, there(c, d))
                        far.wait_send() if finish else far.start()

                    if not finish:

                        @pl.when(d == f)
                        def _():
                            pltpu.make_async_copy(src, dst, sem).start()

    def weight_twin(t):
        block = w_ref.at[pl.ds(pl.multiple_of(c * halves, halves), halves), pl.ds(t * DK, DK)]
        return remote(block, block, w_send.at[4 + t], w_recv.at[3 + t], there(1 - c, f))

    weights(False)
    hops = peers // 2
    for way in range(2):
        ring(way, 1).start()
    first = remote(hid_ref, landing(f, 0, rows), twin_send.at[0], twin_recv.at[0], there(1 - c, f))
    first.start()
    own = pltpu.make_async_copy(hid_ref, landing(f, 0, rows), local)
    own.start()
    gate = pltpu.make_async_copy(gate_ref, w_ref.at[:, pl.ds(3 * DK, DK)], w_local)
    gate.start()
    for hop in range(1, hops + 1):
        for way in range(2):
            ring(way, hop).wait_recv()
            if hop < hops:
                ring(way, hop + 1).start()
            twin(way, hop).start()
        if hop == 1:
            for t in range(2):
                block = w_ref.at[pl.ds(pl.multiple_of(c * halves, halves), halves), pl.ds(t * DK, DK)]
                pltpu.make_async_copy(block, block, w_recv.at[t]).wait()
                weight_twin(t).start()
    block = w_ref.at[:, pl.ds(2 * DK, DK)]
    pltpu.make_async_copy(block, block, w_recv.at[2]).wait()
    own.wait()
    gate.wait()
    first.wait()
    for t in range(2):
        weight_twin(t).wait()
    weights(True)
    for hop in range(1, hops + 1):
        for way in range(2):
            ring(way, hop).wait_send()
            twin(way, hop).wait()


def exchange(hidden_in, qkv_weight, gates):
    rows, width = hidden_in.shape
    anywhere = pl.BlockSpec(memory_space=pl.ANY)
    dma = pltpu.SemaphoreType.DMA
    return pl.pallas_call(
        exchange_kernel,
        in_specs=[anywhere] * 3,
        out_specs=[anywhere] * 2,
        out_shape=[
            jax.ShapeDtypeStruct((2 * HK * rows, width), jnp.bfloat16),
            jax.ShapeDtypeStruct((width, 4 * DK), jnp.bfloat16),
        ],
        scratch_shapes=[dma((2, HK // 2)), dma((2, HK // 2)), dma((HK + 1,)), dma((HK + 1,)), dma, dma((6,)), dma((5,)), dma],
        compiler_params=pltpu.CompilerParams(collective_id=0, has_side_effects=True),
    )(hidden_in, qkv_weight, gates)


def shards(
    hidden_in,
    qkv_weight,
    ab_weight,
    conv_weight,
    decay_rate,
    dt_bias,
    norm_gain,
    previous_tail,
    window_entry_state,
):
    c, f = lax.axis_index("ctx"), lax.axis_index("fsdp")
    own_qk = f % HK
    own = (HV // HK) * own_qk + c
    both = ("ctx", "fsdp")
    gates = jnp.stack(
        [lax.dynamic_index_in_dim(ab_weight, own, 1, False), lax.dynamic_index_in_dim(ab_weight, HV + own, 1, False)],
        axis=1,
    )
    gates = jnp.pad(gates, ((0, 0), (0, DK - 2)))
    if lax.axis_size("fsdp") == HK:
        hidden, weights = exchange(hidden_in, qkv_weight, gates)
    else:
        hidden = lax.all_gather(hidden_in, both, axis=0, tiled=True)
        columns = head_columns(lax.all_gather(qkv_weight, "fsdp", axis=1, tiled=True), own_qk, own)
        weights = jnp.concatenate([columns, gates], axis=1)
    taps = jnp.pad(head_columns(conv_weight, own_qk, own), ((0, 4), (0, 0)))
    tail = jnp.pad(head_columns(previous_tail, own_qk, own).astype(jnp.float32), ((5, 0), (0, 0)))
    take = lambda a: jnp.full((1, DV), lax.dynamic_index_in_dim(a, own, 0, False))
    scal = jnp.concatenate(
        [take(decay_rate), take(dt_bias), norm_gain[None, :], jnp.zeros((5, DV), jnp.float32)], axis=0
    )
    entry = lax.dynamic_index_in_dim(window_entry_state, own, 0, False)
    result = layer(hidden, weights, taps, scal, tail, entry)
    peers = lax.axis_size("ctx") * lax.axis_size("fsdp")
    rows = result.reshape(peers, result.shape[0] // peers, DV)
    swapped = lax.all_to_all(rows, both, 0, 0)
    swapped = swapped.reshape(lax.axis_size("ctx"), lax.axis_size("fsdp"), rows.shape[1], DV)[:, :HK]
    return jnp.transpose(swapped, (2, 1, 0, 3)).reshape(rows.shape[1], HV * DV)


def solution(mesh):
    placed = (
        P(("groups", "ctx", "fsdp"), None),
        P(None, "fsdp"),
        P(),
        P(),
        P(),
        P(),
        P(),
        P("groups", None),
        P("groups", None, None),
    )
    return jax.shard_map(
        shards,
        mesh=mesh,
        in_specs=placed,
        out_specs=P(("groups", "ctx", "fsdp"), None),
        check_vma=False,
    )
```

time: 716 us -> 218 us (0.30)
  the two profiles are of different devices: /device:TPU:31 before, /device:TPU:0 now
where the time goes in v1:
time: 218 us
  Pallas kernels  162 us (74%)
  blocking collectives  43.6 us (20%)
  local copies, waits for them, and re-layouts  10.4 us (5%)
    pallas_call x1, Pallas kernels, exchange(): pl.pallas_call(exchange_kernel, in_specs=[anywhere] * 3, out_specs=[anywh...  123 us
    all_to_all x1, blocking collectives, shards(): swapped = lax.all_to_all(rows, both, 0, 0)  43.6 us
    pallas_call x1, Pallas kernels, layer(): pl.pallas_call(layer_kernel, grid=(tokens // BLOCK,), in_specs=[pl.BlockS...  39.1 us

profile of v1, /device:TPU:0, one launch (start us, length us, event | category | flops | bytes accessed | tf_op | source)
XLA Modules:
  0.0 217.8 jit_solution(10203138124470933601)
XLA Ops:
  0.0 0.0 copy-start
  0.0 1.3 dynamic_slice.42
  1.3 1.2 dynamic_slice.41
  2.6 0.7 constant_dynamic-slice_fusion.2
  3.3 0.7 constant_dynamic-slice_fusion.5
  4.0 0.0 copy-done
  4.0 0.8 constant_dynamic-slice_fusion.7
  4.8 0.3 copy.13
  5.2 1.3 pad_maximum_fusion.1
  6.4 0.1 pad.24.clone
  6.5 0.9 pad.14.gate_ref
  7.4 0.7 maximum_maximum_fusion.scal_ref
  8.2 122.7 %shard_map.91 = (bf16[4096,2048]{1,0:T(8,128)(2,1)}, bf16[2048,512]{1,0:T(8,128)(2,1)}) custom-call(bf16[256,2048]{1,0:T(8,128)(2,1)} %hid_ref.1, bf16[2048,512]{1,0:T(8,128)(2,1)} %shard_ref.1, bf16[2048,128]{1,0:T(8,128)(2,1)} %pad.14.gate_ref), custom_call_target="tpu_custom_call" | custom-call | tf_op jit(solution)/shard_map/pallas_call | solution.py:288
  130.9 0.0 copy-start.1
  130.9 1.6 copy-done.1
  132.5 39.1 %shard_map.92 = bf16[4096,128]{1,0:T(8,128)(2,1)S(1)} custom-call(bf16[4096,2048]{1,0:T(8,128)(2,1)} %get-tuple-element.7.hid_ref, bf16[2048,512]{1,0:T(8,128)(2,1)S(1)} %copy-done.1, f32[8,384]{1,0:T(8,128)S(1)} %select_maximum_fusion.taps_ref, f32[8,128]{1,0:T(8,128)S(1)} %maximum_maximum_fusion.scal_ref, f32[8,384]{1,0:T(8,128)S(1)} %fusion.5.tail_ref, ...), custom_call_target="tpu_custom_call" | custom-call | tf_op jit(solution)/shard_map/pallas_call | solution.py:138
  171.5 43.6 %all_to_all.5 = bf16[16,256,128]{2,1,0:T(8,128)(2,1)S(1)} all-to-all(bf16[16,256,128]{2,1,0:T(8,128)(2,1)S(1)} %bitcast.10), channel_id=1, replica_groups=mesh['groups'=2,'ctx'=2,'fsdp'=8] {'ctx','fsdp'}, dimensions={0} | all-to-all | bytes 2097152 | tf_op jit(solution)/shard_map/all_to_all | solution.py:337
  215.1 1.1 copy.16
  216.2 1.6 reshape.11
  (5 shorter events, 0.0 us)
Async XLA Ops:
  0.0 4.0 %copy-start = (f32[16,128,128]{2,1,0:T(8,128)S(1)}, f32[16,128,128]{2,1,0:T(8,128)}, u32[]{:S(2)}) copy-start(f32[16,128,128]{2,1,0:T(8,128)} %param.17) | copy-start | bytes 3145732
  130.9 1.6 copy-start.1

commit v2 on v1

--- a/solution.py
+++ b/solution.py
@@ -55,8 +55,26 @@
     return inverses
 
 
-def layer_kernel(hid_ref, w_ref, taps_ref, scal_ref, tail_ref, entry_ref, out_ref, buf, state):
+def layer_kernel(hid_ref, w_ref, taps_ref, scal_ref, tail_ref, entry_ref, out_ref, buf, state, *sending):
     step = pl.program_id(0)
+    if sending:
+        held_out, send, recv = sending
+        c, f = lax.axis_index("ctx"), lax.axis_index("fsdp")
+        me, peers = c * HK + f, 2 * HK
+        own = 2 * f + c
+        share = out_ref.shape[0]
+        barrier = pltpu.get_barrier_semaphore()
+
+        @pl.when(step == 0)
+        def _():
+            for away in range(1, peers):
+                other = (me + away) % peers
+                pl.semaphore_signal(
+                    barrier,
+                    inc=1,
+                    device_id={"ctx": other // HK, "fsdp": other % HK},
+                    device_id_type=pl.DeviceIdType.MESH,
+                )
 
     @pl.when(step == 0)
     def _():
@@ -126,24 +144,79 @@
         result = both[CHUNK:] + mm(scores[i], fresh)
         held = ends[i] * held + mm_tn(ks[i], fresh)
         mean_square = jnp.mean(result * result, axis=-1, keepdims=True)
-        out_ref[i * CHUNK : (i + 1) * CHUNK, :] = (
-            result * lax.rsqrt(mean_square + 1e-06) * scal_ref[2:3, :]
-        ).astype(jnp.bfloat16)
+        normed = (result * lax.rsqrt(mean_square + 1e-06) * scal_ref[2:3, :]).astype(jnp.bfloat16)
+        if sending:
+            held_out[pl.ds(pl.multiple_of(step * block + i * CHUNK, CHUNK), CHUNK), :] = normed
+        else:
+            out_ref[i * CHUNK : (i + 1) * CHUNK, :] = normed
     state[...] = held
-
-
-def layer(hidden, weights, taps, scal, tail, entry, interpret=False):
+    if not sending:
+        return
+
+    @pl.when(step == 0)
+    def _():
+        pl.semaphore_wait(barrier, peers - 1)
+
+    def leave(other):
+        return pltpu.make_async_remote_copy(
+            src_ref=held_out.at[pl.ds(pl.multiple_of(other * share, share), share), :],
+            dst_ref=out_ref.at[:, pl.ds(pl.multiple_of(own * DV, DV), DV)],
+            send_sem=send.at[other],
+            recv_sem=recv.at[own],
+            device_id={"ctx": other // HK, "fsdp": other % HK},
+            device_id_type=pl.DeviceIdType.MESH,
+        )
+
+    for at in range(block // share):
+        other = step * (block // share) + at
+
+        @pl.when(other != me)
+        def _():
+            leave(other).start()
+
+        @pl.when(other == me)
+        def _():
+            pltpu.make_async_copy(
+                held_out.at[pl.ds(pl.multiple_of(other * share, share), share), :],
+                out_ref.at[:, pl.ds(pl.multiple_of(own * DV, DV), DV)],
+                recv.at[own],
+            ).start()
+
+    @pl.when(step == pl.num_programs(0) - 1)
+    def _():
+        for other in range(peers):
+            column = out_ref.at[:, pl.ds(other * DV, DV)]
+            pltpu.make_async_copy(column, column, recv.at[other]).wait()
+
+            @pl.when(other != me)
+            def _():
+                leave(other).wait_send()
+
+
+def layer(hidden, weights, taps, scal, tail, entry, direct=False, interpret=False):
     tokens, width = hidden.shape
     full = lambda a: pl.BlockSpec(a.shape, lambda i: (0,) * a.ndim)
+    scratch = [pltpu.VMEM((BLOCK + 8, 3 * DK), jnp.float32), pltpu.VMEM((DK, DV), jnp.float32)]
+    params = dict(vmem_limit_bytes=48 * 1024 * 1024)
+    if direct:
+        peers = 2 * HK
+        out_spec = pl.BlockSpec(memory_space=pl.ANY)
+        out_shape = (tokens // peers, HV * DV)
+        dma = pltpu.SemaphoreType.DMA
+        scratch += [pltpu.VMEM((tokens, DV), jnp.bfloat16), dma((peers,)), dma((peers,))]
+        params.update(collective_id=1, has_side_effects=True)
+    else:
+        out_spec = pl.BlockSpec((BLOCK, DV), lambda i: (i, 0))
+        out_shape = (tokens, DV)
     return pl.pallas_call(
         layer_kernel,
         grid=(tokens // BLOCK,),
         in_specs=[pl.BlockSpec((BLOCK, width), lambda i: (i, 0))]
         + [full(a) for a in (weights, taps, scal, tail, entry)],
-        out_specs=pl.BlockSpec((BLOCK, DV), lambda i: (i, 0)),
-        out_shape=jax.ShapeDtypeStruct((tokens, DV), jnp.bfloat16),
-        scratch_shapes=[pltpu.VMEM((BLOCK + 8, 3 * DK), jnp.float32), pltpu.VMEM((DK, DV), jnp.float32)],
-        compiler_params=pltpu.CompilerParams(vmem_limit_bytes=48 * 1024 * 1024),
+        out_specs=out_spec,
+        out_shape=jax.ShapeDtypeStruct(out_shape, jnp.bfloat16),
+        scratch_shapes=scratch,
+        compiler_params=pltpu.CompilerParams(**params),
         interpret=interpret,
     )(hidden, weights, taps, scal, tail, entry)
 
@@ -161,12 +234,12 @@
 def exchange_kernel(
     hid_ref, shard_ref, gate_ref, all_ref, w_ref, ring_send, ring_recv, twin_send, twin_recv, local, w_send, w_recv, w_local
 ):
-    c, f = lax.axis_index("ctx"), lax.axis_index("fsdp")
+    g, c, f = lax.axis_index("groups"), lax.axis_index("ctx"), lax.axis_index("fsdp")
     peers = HK
     rows = hid_ref.shape[0]
     half = rows // 2
     place = (f // 2) * (1 - f % 2) + (peers - 1 - f // 2) * (f % 2)
-    there = lambda cc, ff: {"ctx": cc, "fsdp": ff}
+    there = lambda cc, ff, gg=g: {"groups": gg, "ctx": cc, "fsdp": ff}
     barrier = pltpu.get_barrier_semaphore()
     for cc in range(2):
         for df in range(peers):
@@ -177,7 +250,11 @@
                     device_id=there((c + cc) % 2, (f + df) % peers),
                     device_id_type=pl.DeviceIdType.MESH,
                 )
-    pl.semaphore_wait(barrier, 2 * peers - 1)
+    for cc in range(2):
+        pl.semaphore_signal(
+            barrier, inc=1, device_id=there((c + cc) % 2, f, 1 - g), device_id_type=pl.DeviceIdType.MESH
+        )
+    pl.semaphore_wait(barrier, 2 * peers + 1)
 
     def remote(src, dst, send, recv, device):
         return pltpu.make_async_remote_copy(
@@ -207,19 +284,20 @@
         at = 1 + way * (peers // 2) + hop - 1
         return remote(block, block, twin_send.at[at], twin_recv.at[at], there(1 - c, f))
 
-    halves = shard_ref.shape[0] // 2
+    quarter = shard_ref.shape[0] // 4
+    lines_qk = pl.ds(pl.multiple_of((2 * g + c) * quarter, quarter), quarter)
+    lines_v = pl.ds(pl.multiple_of(2 * g * quarter, quarter), 2 * quarter)
 
     def weight(i, qk):
         if qk:
             d = (HK // 2) * (f % 2) + i
-            lines = pl.ds(pl.multiple_of(c * halves, halves), halves)
-            src = shard_ref.at[lines, pl.ds(i * DK, DK)]
-            dst = w_ref.at[lines, pl.ds(pl.multiple_of((f // 2) * DK, DK), DK)]
+            src = shard_ref.at[lines_qk, pl.ds(i * DK, DK)]
+            dst = w_ref.at[lines_qk, pl.ds(pl.multiple_of((f // 2) * DK, DK), DK)]
             sem = w_recv.at[f // 2]
         else:
             d = 2 * (f - 4) + i
-            src = shard_ref.at[:, pl.ds(pl.multiple_of((2 * i + c) * DK, DK), DK)]
-            dst = w_ref.at[:, pl.ds(2 * DK, DK)]
+            src = shard_ref.at[lines_v, pl.ds(pl.multiple_of((2 * i + c) * DK, DK), DK)]
+            dst = w_ref.at[lines_v, pl.ds(2 * DK, DK)]
             sem = w_recv.at[2]
         return d, src, dst, sem
 
@@ -242,9 +320,14 @@
                         def _():
                             pltpu.make_async_copy(src, dst, sem).start()
 
-    def weight_twin(t):
-        block = w_ref.at[pl.ds(pl.multiple_of(c * halves, halves), halves), pl.ds(t * DK, DK)]
-        return remote(block, block, w_send.at[4 + t], w_recv.at[3 + t], there(1 - c, f))
+    blocks = [w_ref.at[lines_qk, pl.ds(t * DK, DK)] for t in range(2)] + [w_ref.at[lines_v, pl.ds(2 * DK, DK)]]
+    others = ((0, 1), (1, 0), (1, 1))
+
+    def weight_shares():
+        for t in range(3):
+            for at, (dg, dc) in enumerate(others if t < 2 else others[1:2]):
+                sem = 4 + 3 * t + at
+                yield remote(blocks[t], blocks[t], w_send.at[sem], w_recv.at[sem], there((c + dc) % 2, f, (g + dg) % 2))
 
     weights(False)
     hops = peers // 2
@@ -263,17 +346,15 @@
                 ring(way, hop + 1).start()
             twin(way, hop).start()
         if hop == 1:
-            for t in range(2):
-                block = w_ref.at[pl.ds(pl.multiple_of(c * halves, halves), halves), pl.ds(t * DK, DK)]
-                pltpu.make_async_copy(block, block, w_recv.at[t]).wait()
-                weight_twin(t).start()
-    block = w_ref.at[:, pl.ds(2 * DK, DK)]
-    pltpu.make_async_copy(block, block, w_recv.at[2]).wait()
+            for t in range(3):
+                pltpu.make_async_copy(blocks[t], blocks[t], w_recv.at[t]).wait()
+            for share in weight_shares():
+                share.start()
     own.wait()
     gate.wait()
     first.wait()
-    for t in range(2):
-        weight_twin(t).wait()
+    for share in weight_shares():
+        share.wait()
     weights(True)
     for hop in range(1, hops + 1):
         for way in range(2):
@@ -293,7 +374,7 @@
             jax.ShapeDtypeStruct((2 * HK * rows, width), jnp.bfloat16),
             jax.ShapeDtypeStruct((width, 4 * DK), jnp.bfloat16),
         ],
-        scratch_shapes=[dma((2, HK // 2)), dma((2, HK // 2)), dma((HK + 1,)), dma((HK + 1,)), dma, dma((6,)), dma((5,)), dma],
+        scratch_shapes=[dma((2, HK // 2)), dma((2, HK // 2)), dma((HK + 1,)), dma((HK + 1,)), dma, dma((11,)), dma((11,)), dma],
         compiler_params=pltpu.CompilerParams(collective_id=0, has_side_effects=True),
     )(hidden_in, qkv_weight, gates)
 
@@ -318,7 +399,8 @@
         axis=1,
     )
     gates = jnp.pad(gates, ((0, 0), (0, DK - 2)))
-    if lax.axis_size("fsdp") == HK:
+    direct = lax.axis_size("fsdp") == HK and lax.axis_size("groups") == 2
+    if direct:
         hidden, weights = exchange(hidden_in, qkv_weight, gates)
     else:
         hidden = lax.all_gather(hidden_in, both, axis=0, tiled=True)
@@ -331,7 +413,9 @@
         [take(decay_rate), take(dt_bias), norm_gain[None, :], jnp.zeros((5, DV), jnp.float32)], axis=0
     )
     entry = lax.dynamic_index_in_dim(window_entry_state, own, 0, False)
-    result = layer(hidden, weights, taps, scal, tail, entry)
+    result = layer(hidden, weights, taps, scal, tail, entry, direct)
+    if direct:
+        return result
     peers = lax.axis_size("ctx") * lax.axis_size("fsdp")
     rows = result.reshape(peers, result.shape[0] // peers, DV)
     swapped = lax.all_to_all(rows, both, 0, 0)

time: 218 us -> 170 us (0.78)
  the two profiles are of different devices: /device:TPU:0 before, /device:TPU:31 now
where the time goes in v2:
time: 170 us; the launch traced here: 169 us
  Pallas kernels  159 us (94%)
  local copies, waits for them, and re-layouts  8.66 us (5%)
  other arithmetic  2.05 us (1%)
    pallas_call x1, Pallas kernels, exchange(): pl.pallas_call(exchange_kernel, in_specs=[anywhere] * 3, out_specs=[anywh...  110 us
    pallas_call x1, Pallas kernels, layer(): pl.pallas_call(layer_kernel, grid=(tokens // BLOCK,), in_specs=[pl.BlockS...  48.8 us

profile of v2, /device:TPU:31, one launch (start us, length us, event | category | flops | bytes accessed | tf_op | source)
XLA Modules:
  0.0 169.3 jit_solution(11051107616004331141)
XLA Ops:
  0.0 0.0 copy-start
  0.0 1.3 dynamic_slice.42
  1.3 1.2 dynamic_slice.41
  2.6 1.3 pad_maximum_fusion.1
  3.8 0.1 pad.24.clone
  3.9 0.7 maximum_maximum_fusion.scal_ref
  4.6 0.7 constant_dynamic-slice_fusion.2
  5.4 0.7 constant_dynamic-slice_fusion.5
  6.1 0.8 constant_dynamic-slice_fusion.7
  6.9 0.0 copy-done
  7.0 0.3 copy.12
  7.3 0.9 pad.14.gate_ref
  8.2 109.7 %shard_map.91 = (bf16[4096,2048]{1,0:T(8,128)(2,1)}, bf16[2048,512]{1,0:T(8,128)(2,1)}) custom-call(bf16[256,2048]{1,0:T(8,128)(2,1)} %hid_ref.1, bf16[2048,512]{1,0:T(8,128)(2,1)} %shard_ref.1, bf16[2048,128]{1,0:T(8,128)(2,1)} %pad.14.gate_ref), custom_call_target="tpu_custom_call" | custom-call | tf_op jit(solution)/shard_map/pallas_call | solution.py:369
  117.9 0.0 copy-start.1
  117.9 1.6 copy-done.1
  119.5 48.8 %shard_map.92 = bf16[256,2048]{1,0:T(8,128)(2,1)S(1)} custom-call(bf16[4096,2048]{1,0:T(8,128)(2,1)} %get-tuple-element.7.hid_ref, bf16[2048,512]{1,0:T(8,128)(2,1)S(1)} %copy-done.1, f32[8,384]{1,0:T(8,128)S(1)} %select_maximum_fusion.taps_ref, f32[8,128]{1,0:T(8,128)S(1)} %maximum_maximum_fusion.scal_ref, f32[8,384]{1,0:T(8,128)S(1)} %fusion.5.tail_ref, ...), custom_call_target="tpu_custom_call" | custom-call | tf_op jit(solution)/shard_map/pallas_call | solution.py:211
  168.3 1.0 copy.14
  (5 shorter events, 0.1 us)
Async XLA Ops:
  0.0 6.9 %copy-start = (f32[16,128,128]{2,1,0:T(8,128)S(1)}, f32[16,128,128]{2,1,0:T(8,128)}, u32[]{:S(2)}) copy-start(f32[16,128,128]{2,1,0:T(8,128)} %param.17) | copy-start | bytes 3145732
  117.9 1.6 copy-start.1

commit v3 on v2

--- a/solution.py
+++ b/solution.py
@@ -9,7 +9,7 @@
 HV = 16
 DK = 128
 DV = 128
-BLOCK = 512
+BLOCK = 1024
 CHUNK = 128
 BASE = 32
 
@@ -394,11 +394,10 @@
     own_qk = f % HK
     own = (HV // HK) * own_qk + c
     both = ("ctx", "fsdp")
-    gates = jnp.stack(
-        [lax.dynamic_index_in_dim(ab_weight, own, 1, False), lax.dynamic_index_in_dim(ab_weight, HV + own, 1, False)],
-        axis=1,
-    )
-    gates = jnp.pad(gates, ((0, 0), (0, DK - 2)))
+    line = lax.broadcasted_iota(jnp.int32, (2 * HV, DK), 0)
+    column = lax.broadcasted_iota(jnp.int32, (2 * HV, DK), 1)
+    chosen = (line == own + HV * column) & (column < 2)
+    gates = jnp.dot(ab_weight, chosen.astype(jnp.bfloat16), preferred_element_type=jnp.float32).astype(jnp.bfloat16)
     direct = lax.axis_size("fsdp") == HK and lax.axis_size("groups") == 2
     if direct:
         hidden, weights = exchange(hidden_in, qkv_weight, gates)

time: 170 us -> 164 us (0.965)
  Pallas kernels: 159 us -> 153 us
  matrix products: 0 us -> 2.05 us
  local copies, waits for them, and re-layouts: 8.66 us -> 6.66 us
    pallas_call x1, Pallas kernels: 48.8 us -> 43.5 us  [layer(): pl.pallas_call(layer_kernel, grid=(tokens // BLOCK,), in_specs=[pl.BlockS...]
    dot_general x0 -> x1, matrix products: none -> 2.05 us  [shards(): jnp.dot(ab_weight, chosen.astype(jnp.bfloat16), preferred_element_type=jn...]
where the time goes in v3:
time: 164 us
  Pallas kernels  153 us (93%)
  local copies, waits for them, and re-layouts  6.66 us (4%)
  other arithmetic  2.09 us (1%)
  matrix products  2.05 us (1%)
    pallas_call x1, Pallas kernels, exchange(): pl.pallas_call(exchange_kernel, in_specs=[anywhere] * 3, out_specs=[anywh...  110 us
    pallas_call x1, Pallas kernels, layer(): pl.pallas_call(layer_kernel, grid=(tokens // BLOCK,), in_specs=[pl.BlockS...  43.5 us

profile of v3, /device:TPU:31, one launch (start us, length us, event | category | flops | bytes accessed | tf_op | source)
XLA Modules:
  0.0 164.0 jit_solution(12362749559012230049)
XLA Ops:
  0.0 0.0 copy-start
  0.0 1.3 dynamic_slice.33
  1.3 1.2 dynamic_slice.32
  2.6 1.3 pad_maximum_fusion
  3.9 0.1 pad.19.clone
  4.0 0.7 maximum_maximum_fusion.scal_ref
  4.7 0.7 constant_dynamic-slice_fusion.2
  5.5 0.7 constant_dynamic-slice_fusion.5
  6.2 0.0 copy-done
  6.2 2.1 %fusion.gate_ref = bf16[2048,128]{1,0:T(8,128)(2,1)} fusion(bf16[2048,32]{0,1:T(8,128)(2,1)} %param.11, s32[128]{0:T(128)S(1)} %multiply_add_fusion, pred[128]{0:T(512)(128)(4,1)S(1)} %iota_compare_fusion.3), kind=kOutput, calls=%fused_computation.1 | convolution fusion | flops 17047552 | bytes 656000 | tf_op jit(solution)/shard_map/dot_general | solution.py:400
  8.3 109.7 %shard_map.91 = (bf16[4096,2048]{1,0:T(8,128)(2,1)}, bf16[2048,512]{1,0:T(8,128)(2,1)}) custom-call(bf16[256,2048]{1,0:T(8,128)(2,1)} %hid_ref.1, bf16[2048,512]{1,0:T(8,128)(2,1)} %shard_ref.1, bf16[2048,128]{1,0:T(8,128)(2,1)} %fusion.gate_ref), custom_call_target="tpu_custom_call" | custom-call | tf_op jit(solution)/shard_map/pallas_call | solution.py:369
  118.0 0.0 copy-start.1
  118.0 1.6 copy-done.1
  119.6 43.5 %shard_map.92 = bf16[256,2048]{1,0:T(8,128)(2,1)S(1)} custom-call(bf16[4096,2048]{1,0:T(8,128)(2,1)} %get-tuple-element.7.hid_ref, bf16[2048,512]{1,0:T(8,128)(2,1)S(1)} %copy-done.1, f32[8,384]{1,0:T(8,128)S(1)} %select_maximum_fusion.taps_ref, f32[8,128]{1,0:T(8,128)S(1)} %maximum_maximum_fusion.scal_ref, f32[8,384]{1,0:T(8,128)S(1)} %fusion.10.tail_ref, ...), custom_call_target="tpu_custom_call" | custom-call | tf_op jit(solution)/shard_map/pallas_call | solution.py:211
  163.0 1.0 copy.13
  (6 shorter events, 0.0 us)
Async XLA Ops:
  0.0 6.2 %copy-start = (f32[16,128,128]{2,1,0:T(8,128)S(1)}, f32[16,128,128]{2,1,0:T(8,128)}, u32[]{:S(2)}) copy-start(f32[16,128,128]{2,1,0:T(8,128)} %param.17) | copy-start | bytes 3145732
  118.0 1.6 copy-start.1
